TPU v7x, 128 devices: a whole 4x4x4 slice. The times are simulated.
128 devices in a mesh: grid: 16 (over z_lo, y, core), mode: 8 (over z_hi, x).
Axes of the slice: x: 4, y: 4, z: 4 (z_hi: 2, z_lo: 2; z = z_hi * 2 + z_lo), core: 2. Of those that a mesh axis runs over, the one named last changes fastest.
Arguments:
- pod_basis: bfloat16 [524288, 2048], P('grid', 'mode'), may hold values from -0.125 to 0.125
- probe_vectors: float32 [16, 2048], P(None, 'mode'), may hold values from -6 to 6
- drifter_tiles: int32 [16, 4096], P('grid'), may hold values from 0 to 4095, as said below
- tile_counts: int32 [4096], P('grid'), may hold values from 0 to 32, as said below
- stencil_offsets: int32 [4, 16, 4096], P(None, 'grid'), may hold values from 0 to 127
- stencil_weights: float32 [4, 16, 4096], P(None, 'grid'), may hold values from 0.05 to 0.5
- error_scales: float32 [16, 4096], P('grid'), may hold values from 1 to 6
- time_precision: float32 [16, 16], replicated, as said below
Outputs:
- first_product: float32 [16, 2048], P(None, 'mode')
- second_product: float32 [16, 2048], P(None, 'mode')
Inputs may be any that keep to these rules, and one draw needn't show every extreme that they name: drifter_tiles[k, j] is a tile of window k, from k * 256 to (k + 1) * 256 - 1; no tile holds more than 32 drifters. tile_counts[t] is the number of entries of drifter_tiles equal to t. `time_precision`: symmetric, every diagonal entry 1, off-diagonal magnitudes of a row sum to less than 1.
All inputs are finite; a program needn't handle non-finite values.
Results may differ from a plain program's by a relative error of at most 0.0029.
The roundings to bfloat16 on the way count: a program that leaves them out, or rounds other values in their place, can miss the bound.
Values may be sent and summed in bfloat16 or wider, within the bound.
A program may use at most 128 MiB of HBM per device.

v0:
```python
import jax
import jax.numpy as jnp
from jax import lax
from jax.sharding import PartitionSpec as P

TILE = 128


def local(
    pod_basis,
    probe_vectors,
    drifter_tiles,
    tile_counts,
    stencil_offsets,
    stencil_weights,
    error_scales,
    time_precision,
):
    window = lax.axis_index("grid")
    tile_total = tile_counts.shape[0]
    local_tile = drifter_tiles[0] - window * tile_total
    tile_match = (local_tile[:, None] == jnp.arange(tile_total, dtype=jnp.int32)[None, :]).astype(
        jnp.float32
    )
    tile_count = jnp.dot(
        tile_match, tile_counts.astype(jnp.float32), precision=lax.Precision.HIGHEST
    )
    obs_gain = error_scales[0] / jnp.sqrt(tile_count)
    point_rows = local_tile[None, :] * TILE + stencil_offsets[:, 0, :]
    prec_row = lax.dynamic_slice_in_dim(time_precision, window, 1, 0)[0]
    row_span = pod_basis.shape[0]
    inside = (point_rows >= 0) & (point_rows < row_span)
    safe_rows = jnp.clip(point_rows, 0, row_span - 1)
    live_weight = jnp.where(inside, stencil_weights[:, 0, :], 0.0)
    probe_count = probe_vectors.shape[0]

    def accumulate(shard_part):
        return jnp.einsum("l,lpd->pd", prec_row, shard_part, precision=lax.Precision.HIGHEST)

    def hessian(vector):
        probe_bf = vector.astype(jnp.bfloat16)
        state_rows = lax.dot_general(
            probe_bf, pod_basis, (((1,), (1,)), ((), ())), preferred_element_type=jnp.float32
        )
        scaled = obs_gain[None] * jnp.sum(live_weight[None] * state_rows[:, safe_rows], axis=1)
        scaled = lax.psum(scaled, "mode")
        coupled = accumulate(lax.all_gather(scaled[None], "grid", axis=0, tiled=True))
        weighted = obs_gain[None] * coupled
        spread = (live_weight[None] * weighted[:, None, :]).reshape(probe_count, -1)
        adjoint = (
            jnp.zeros((probe_count, row_span), jnp.float32).at[:, safe_rows.reshape(-1)].add(spread)
        )
        adjoint_bf = adjoint.astype(jnp.bfloat16)
        partial_back = lax.dot_general(
            adjoint_bf, pod_basis, (((1,), (0,)), ((), ())), preferred_element_type=jnp.float32
        )
        increment = lax.psum(partial_back, "grid")
        return vector + increment

    first_product = hessian(probe_vectors)
    second_product = hessian(first_product)
    return (first_product, second_product)


def solution(mesh):
    return jax.shard_map(
        local,
        mesh=mesh,
        in_specs=(
            P("grid", "mode"),
            P(None, "mode"),
            P("grid", None),
            P("grid"),
            P(None, "grid", None),
            P(None, "grid", None),
            P("grid", None),
            P(),
        ),
        out_specs=(P(None, "mode"), P(None, "mode")),
        check_vma=False,
    )
```

profile of v0, /device:TPU:1, one launch (start us, length us, event | category | flops | bytes accessed | tf_op | source)
XLA Modules:
  0.0 782.5 jit_solution(5647968045078398808)
XLA Ops:
  7.2 0.0 copy-start
  7.2 0.0 all-reduce.3.cloned.1.call-start
  7.2 0.7 convert_element_type.16
  7.9 0.7 broadcast_multiply_fusion
  8.7 1.0 compare_select_fusion
  9.6 1.0 bitcast_select_fusion
  10.6 2.1 fusion.14
  12.8 0.7 rsqrt_multiply_fusion
  13.5 16.0 %fusion.19 = f32[16,32768]{0,1:T(8,128)} fusion(bf16[32768,256]{1,0:T(8,128)(2,1)} %param.8, f32[16,256]{1,0:T(8,128)} %param.9), kind=kOutput, calls=%fused_computation.42 | convolution fusion | flops 268439552 | bytes 18890752 | tf_op jit(solution)/shard_map/dot_general | solution.py:42
  29.5 60.2 %gather_fusion = f32[16384,16]{1,0:T(8,128)} fusion(f32[16,32768]{0,1:T(8,128)} %fusion.19, s32[16384]{0:T(1024)S(1)} %broadcast_clamp_fusion), kind=kCustom, calls=%fused_computation | custom fusion | bytes 2162688 | tf_op jit(solution)/shard_map/gather | solution.py:45
  89.7 0.0 copy-start.1
  89.7 0.0 copy-start.2
  89.7 5.4 multiply_reduce_fusion.1
  95.1 1.9 multiply_bitcast_fusion.1
  97.0 0.0 all-reduce.3.cloned.1.call-update
  97.0 0.0 all-gather.3.cloned.1.call-start
  97.0 91.4 %all-reduce.3.cloned.1.call-done = f32[1,16,4096]{1,2,0:T(8,128)} async-done(((f32[1,16,4096]{1,2,0:T(8,128)}), f32[1,16,4096]{1,2,0:T(8,128)}) %all-reduce.3.cloned.1.call-update) | async-done | bytes 262160 | tf_op jit(solution)/shard_map/psum | solution.py:46
  188.4 2.9 copy.15
  191.3 0.0 all-gather.3.cloned.1.call-update
  191.3 0.6 all-reduce.5.cloned.1.call-start
  191.9 0.1 copy.26
  192.0 0.0 copy-done.1
  192.0 0.0 copy-done.2
  192.1 0.1 compare_select_fusion.1
  192.2 40.4 %all-gather.3.cloned.1.call-done = f32[16,16,4096]{2,1,0:T(8,128)} async-done(((f32[1,16,4096]{2,1,0:T(8,128)}), f32[16,16,4096]{2,1,0:T(8,128)}) %all-gather.3.cloned.1.call-update) | async-done | bytes 4194320 | tf_op jit(solution)/shard_map/all_gather | solution.py:47
  232.6 0.0 copy-done
  232.6 6.4 fusion.12
  239.1 0.8 copy.20
  239.8 0.6 bitcast_multiply_fusion.3
  240.4 4.4 bitcast_multiply_fusion.1
  244.8 86.6 %scatter_custom_fusion = f32[16,32768]{0,1:T(8,128)} fusion(s32[16384]{0:T(1024)S(1)} %bitcast.78, f32[16,16384]{0,1:T(8,128)} %bitcast_multiply_fusion.1, f32[]{:T(128)} %constant.9.clone.1), kind=kCustom, calls=%fused_computation.7 | custom fusion | flops 262144 | bytes 3145732 | tf_op jit(solution)/shard_map/scatter-add | solution.py:51
  331.4 0.0 copy-start.4
  331.4 12.8 %fusion.6 = f32[16,256]{1,0:T(8,128)S(1)} fusion(bf16[32768,256]{1,0:T(8,128)(2,1)} %param.8, f32[16,32768]{0,1:T(8,128)} %scatter_custom_fusion), kind=kOutput, calls=%fused_computation.14 | convolution fusion | flops 268959744 | bytes 18890752 | tf_op jit(solution)/shard_map/dot_general | solution.py:54
  344.3 50.5 %psum.29 = f32[16,256]{1,0:T(8,128)S(1)} all-reduce(f32[16,256]{1,0:T(8,128)S(1)} %fusion.6), channel_id=1, replica_groups=mesh['grid'=16,'mode'=8] {'grid'}, use_global_device_ids=true, to_apply=%region_3.4 | all-reduce | flops 4096 | bytes 32768 | tf_op jit(solution)/shard_map/psum | solution.py:57
  394.8 0.0 copy-done.4
  394.8 0.0 copy-start.3
  394.8 16.0 %fusion.17 = f32[16,32768]{0,1:T(8,128)} fusion(bf16[32768,256]{1,0:T(8,128)(2,1)} %param.8, f32[16,256]{1,0:T(8,128)S(1)} %add.97), kind=kOutput, calls=%fused_computation.40 | convolution fusion | flops 268439552 | bytes 18890752 | tf_op jit(solution)/shard_map/dot_general | solution.py:42
  410.8 60.2 %gather_fusion.1 = f32[16384,16]{1,0:T(8,128)} fusion(f32[16,32768]{0,1:T(8,128)} %fusion.17, s32[16384]{0:T(1024)S(1)} %broadcast_clamp_fusion), kind=kCustom, calls=%fused_computation.1 | custom fusion | bytes 2162688 | tf_op jit(solution)/shard_map/gather | solution.py:45
  471.0 5.4 multiply_reduce_fusion
  476.3 1.9 multiply_bitcast_fusion
  478.2 0.0 all-reduce.5.cloned.1.call-update
  478.3 0.3 all-gather.5.cloned.1.call-start
  478.5 90.2 %all-reduce.5.cloned.1.call-done = f32[1,16,4096]{1,2,0:T(8,128)} async-done(((f32[1,16,4096]{1,2,0:T(8,128)}), f32[1,16,4096]{1,2,0:T(8,128)}) %all-reduce.5.cloned.1.call-update) | async-done | bytes 262160 | tf_op jit(solution)/shard_map/psum | solution.py:46
  568.7 2.9 copy.17
  571.6 0.0 all-gather.5.cloned.1.call-update
  571.6 41.3 %all-gather.5.cloned.1.call-done = f32[16,16,4096]{2,1,0:T(8,128)} async-done(((f32[1,16,4096]{2,1,0:T(8,128)}), f32[16,16,4096]{2,1,0:T(8,128)}) %all-gather.5.cloned.1.call-update) | async-done | bytes 4194320 | tf_op jit(solution)/shard_map/all_gather | solution.py:47
  612.9 6.4 fusion.10
  619.4 0.8 copy.23
  620.1 0.6 bitcast_multiply_fusion.2
  620.7 4.4 bitcast_multiply_fusion
  625.1 86.7 %scatter_custom_fusion.1 = f32[16,32768]{0,1:T(8,128)} fusion(s32[16384]{0:T(1024)S(1)} %bitcast.79, f32[16,16384]{0,1:T(8,128)} %bitcast_multiply_fusion, f32[]{:T(128)} %constant.9.clone.1), kind=kCustom, calls=%fused_computation.4 | custom fusion | flops 262144 | bytes 3145732 | tf_op jit(solution)/shard_map/scatter-add | solution.py:51
  711.8 12.8 %fusion.4 = f32[16,256]{1,0:T(8,128)S(1)} fusion(bf16[32768,256]{1,0:T(8,128)(2,1)} %param.8, f32[16,32768]{0,1:T(8,128)} %scatter_custom_fusion.1), kind=kOutput, calls=%fused_computation.12 | convolution fusion | flops 268959744 | bytes 18890752 | tf_op jit(solution)/shard_map/dot_general | solution.py:54
  724.6 50.5 %psum.31 = f32[16,256]{1,0:T(8,128)S(1)} all-reduce(f32[16,256]{1,0:T(8,128)S(1)} %fusion.4), channel_id=1, replica_groups=mesh['grid'=16,'mode'=8] {'grid'}, use_global_device_ids=true, to_apply=%region_7.8 | all-reduce | flops 4096 | bytes 32768 | tf_op jit(solution)/shard_map/psum | solution.py:57
  775.1 0.0 copy-done.3
  775.1 0.6 add.98
  (5 shorter events, 0.1 us)
Async XLA Ops:
  7.2 225.5 %copy-start = (f32[16,16]{1,0:T(8,128)S(1)}, f32[16,16]{1,0:T(8,128)}, u32[]{:S(2)}) copy-start(f32[16,16]{1,0:T(8,128)} %param.15) | copy-start | bytes 3076
  7.2 181.3 %all-reduce.3.cloned.1.call-start = ((), (), s32[]{:S(2)}) async-start(), calls=%async_computation | async-start | bytes 4194304 | tf_op jit(solution)/shard_map/psum | solution.py:46
  89.7 102.3 %copy-start.1 = (s32[4,1,4096]{2,1,0:T(1,128)S(1)}, s32[4,1,4096]{2,1,0:T(1,128)}, u32[]{:S(2)}) copy-start(s32[4,1,4096]{2,1,0:T(1,128)} %param.12) | copy-start | bytes 196612
  89.7 102.3 %copy-start.2 = (f32[4,1,4096]{2,1,0:T(1,128)S(1)}, f32[4,1,4096]{2,1,0:T(1,128)}, u32[]{:S(2)}) copy-start(f32[4,1,4096]{2,1,0:T(1,128)} %param.13) | copy-start | bytes 196612
  97.0 135.6 %all-gather.3.cloned.1.call-start = ((), (), s32[]{:S(2)}) async-start(), calls=%async_computation.1 | async-start | bytes 4456448 | tf_op jit(solution)/shard_map/all_gather | solution.py:47
  191.3 377.4 %all-reduce.5.cloned.1.call-start = ((), (), s32[]{:S(2)}) async-start(), calls=%async_computation.2 | async-start | bytes 4194304 | tf_op jit(solution)/shard_map/psum | solution.py:46
  331.4 63.4 %copy-start.4 = (f32[16,256]{1,0:T(8,128)S(1)}, f32[16,256]{1,0:T(8,128)}, u32[]{:S(2)}) copy-start(f32[16,256]{1,0:T(8,128)} %param.9) | copy-start | bytes 49156
  394.8 380.3 %copy-start.3 = (f32[16,256]{1,0:T(8,128)}, f32[16,256]{1,0:T(8,128)S(1)}, u32[]{:S(2)}) copy-start(f32[16,256]{1,0:T(8,128)S(1)} %add.97) | copy-start | bytes 49156
  478.3 134.7 %all-gather.5.cloned.1.call-start = ((), (), s32[]{:S(2)}) async-start(), calls=%async_computation.3 | async-start | bytes 4456448 | tf_op jit(solution)/shard_map/all_gather | solution.py:47
Sparse Core Ops, SparseCore 0:
  97.1 91.2 all-reduce.2
  191.4 41.1 all-gather.2
  478.4 90.3 all-reduce.4
  571.7 41.1 all-gather.4
where the time goes:
time: 792 us; the launch traced here: 783 us
  waiting for transfers between devices  263 us (33%)
  other arithmetic  203 us (26%)
  local copies, waits for them, and re-layouts  128 us (16%)
  blocking collectives  101 us (13%)
  matrix products  72.6 us (9%)
  between operations  14.2 us (2%)
    psum x2, waiting for transfers between devices, hessian(): scaled = lax.psum(scaled, 'mode')  182 us
    scatter-add x2, other arithmetic, hessian(): jnp.zeros((probe_count, row_span), jnp.float32).at[:, safe_rows.reshape(-1)]  173 us
    gather x2, local copies, waits for them, and re-layouts, hessian(): state_rows[:, safe_rows]  120 us
    psum x2, blocking collectives, hessian(): increment = lax.psum(partial_back, 'grid')  101 us
    all_gather x2, waiting for transfers between devices, hessian(): lax.all_gather(scaled[None], 'grid', axis=0, tiled=True)  81.7 us
    dot_general x2, matrix products, hessian(): lax.dot_general(probe_bf, pod_basis, (((1,), (1,)), ((), ())), preferred_...  32 us
    dot_general x2, matrix products, hessian(): lax.dot_general(adjoint_bf, pod_basis, (((1,), (0,)), ((), ())), preferre...  25.7 us
  transfers between devices with their start and end apart: 4, of which 4 were waited for; matrix products, arithmetic and copies ran while one was open for 0% of the time, Pallas kernels for 0%

commit v1 on v0

v1 whole, which is shorter than its diff:
```python
import functools

import jax
import jax.numpy as jnp
from jax import lax
from jax.experimental import pallas as pl
from jax.experimental.pallas import tpu as pltpu
from jax.sharding import PartitionSpec as P

F32 = jnp.float32
BF16 = jnp.bfloat16
I32 = jnp.int32
MESH = pl.DeviceIdType.MESH

LOADS = 16
PARTS = 4
PART_H = 16

NN = (((1,), (0,)), ((), ()))
NT = (((1,), (1,)), ((), ()))


def mm(a, b, dims):
    return lax.dot_general(a, b, dims, preferred_element_type=F32)


def lanes_of(x, idx):
    return jnp.take_along_axis(x, idx, axis=1, mode="promise_in_bounds")


def kernel(
    n_grid,
    n_mode,
    basis,
    probe,
    tiles,
    counts,
    offs,
    wts,
    scales,
    prec,
    out1,
    out2,
    B,
    WT,
    offS,
    wS,
    jrowS,
    jlaneS,
    hiJ,
    loJ,
    gainJ,
    packJ,
    partial,
    rs_in,
    X,
    Z,
    R,
    C,
    D,
    S,
    Fw,
    acc_out,
    ar_in,
    vec,
    load_sem,
    rs_send,
    rs_recv,
    a1_send,
    a1_recv,
    a2_send,
    a2_recv,
    ag_send,
    ag_recv,
    ar_send,
    ar_recv,
):
    g = lax.axis_index("grid")
    m = lax.axis_index("mode")
    rows = basis.shape[0] // LOADS

    def load(i):
        return pltpu.make_async_copy(
            basis.at[pl.ds(i * rows, rows)], B.at[pl.ds(i * rows, rows)], load_sem.at[i]
        )

    for i in range(LOADS):
        load(i).start()

    barrier = pltpu.get_barrier_semaphore()
    for d in range(1, n_mode):
        pl.semaphore_signal(
            barrier, inc=1, device_id=(g, lax.rem(m + d, n_mode)), device_id_type=MESH
        )
    for d in range(1, n_grid):
        pl.semaphore_signal(
            barrier, inc=1, device_id=(lax.rem(g + d, n_grid), m), device_id_type=MESH
        )

    sub = lax.broadcasted_iota(I32, (256, 256), 0)
    lan = lax.broadcasted_iota(I32, (256, 256), 1)
    upto = (sub <= lan).astype(BF16)
    ones = jnp.ones((16, 256), BF16)
    base = jnp.zeros((16, 256), F32)
    first = lax.broadcasted_iota(I32, (16, 256), 0) == 0
    count_row = jnp.broadcast_to(counts[...].astype(F32), (16, 256))
    inverse = jnp.zeros((64, 256), F32)
    hsub = lax.broadcasted_iota(I32, (64, 256), 0)
    lsub = lax.broadcasted_iota(I32, (128, 256), 0)
    jlan = lax.broadcasted_iota(I32, (1, 256), 1)
    for b in range(16):
        cols = pl.ds(b * 256, 256)
        lt = tiles[0:1, cols] - g * 256
        onehot = (sub == lt).astype(F32)
        onehot_bf = onehot.astype(BF16)
        within = mm(onehot_bf, upto, NN)
        looked = mm(jnp.where(first, base, count_row).astype(BF16), onehot_bf, NN)
        rank = jnp.sum(onehot * within, axis=0, keepdims=True) + looked[0:1] - 1.0
        base = base + mm(ones, onehot_bf, NT)
        gain = scales[0:1, cols] / jnp.sqrt(looked[1:2])
        hi = lt >> 2
        lo = (lt & 3) * 32 + rank.astype(I32)
        packed = offs[0, 0:1, cols]
        for s in range(1, 4):
            packed = packed | (offs[s, 0:1, cols] << (7 * s))
        for r in range(2):
            row = pl.ds(2 * b + r, 1)
            hiJ[row, :] = hi[:, 128 * r : 128 * r + 128]
            loJ[row, :] = lo[:, 128 * r : 128 * r + 128]
            gainJ[row, :] = gain[:, 128 * r : 128 * r + 128]
            packJ[row, :] = packed[:, 128 * r : 128 * r + 128]
        j = jlan + b * 256
        low = lsub == lo
        jrow1 = jnp.where(low, ((j >> 7) + 1).astype(F32), 0.0).astype(BF16)
        jlane = jnp.where(low, (j & 127).astype(F32), 0.0).astype(BF16)
        high = (hsub == hi).astype(F32).astype(BF16)
        inverse = inverse + mm(high, jnp.concatenate([jrow1, jlane], axis=0), NT)
    jrowS[...] = inverse[:, :128].astype(I32) - 1
    jlaneS[...] = inverse[:, 128:].astype(I32)

    for half in range(2):
        at = [32 * half + 8 * i for i in range(4)]
        want = [jrowS[a : a + 8, :] for a in at]
        lane = [jlaneS[a : a + 8, :] for a in at]

        def place(r, got):
            src = [packJ[pl.ds(r, 1), :]]
            src += [wts[s, 0:1, pl.ds(pl.multiple_of(r * 128, 128), 128)] for s in range(4)]
            src = [jnp.broadcast_to(x, (8, 128)) for x in src]
            new = []
            for i in range(4):
                here = want[i] == r
                for k in range(5):
                    new.append(jnp.where(here, lanes_of(src[k], lane[i]), got[5 * i + k]))
            return tuple(new)

        zero = [jnp.zeros((8, 128), I32)] + [jnp.zeros((8, 128), F32)] * 4
        got = lax.fori_loop(0, 32, place, tuple(zero * 4), unroll=2)
        for i in range(4):
            for s in range(4):
                offS[s, pl.ds(at[i], 8), :] = (got[5 * i] >> (7 * s)) & 127
                wS[s, pl.ds(at[i], 8), :] = got[5 * i + 1 + s]

    def stencil_matrix(h, carry):
        point = lax.broadcasted_iota(I32, (128, 128), 0)
        w = jnp.zeros((128, 128), F32)
        for s in range(4):
            w = w + jnp.where(point == offS[s, pl.ds(h, 1), :], wS[s, pl.ds(h, 1), :], 0.0)
        w_hi = w.astype(BF16)
        w_lo = (w - w_hi.astype(F32)).astype(BF16)
        at = pl.multiple_of(h * 128, 128)
        WT[pl.ds(at, 128), 0:128] = w_hi
        WT[pl.ds(at, 128), 128:256] = w_lo
        return carry

    vec[...] = probe[...]
    lane_group = lax.broadcasted_iota(I32, (8, 128), 1) >> 5
    group16 = lax.broadcasted_iota(I32, (16, 128), 1) >> 5

    def hessian(t, out):
        v_bf = vec[...].astype(BF16)

        def state(h):
            at = pl.multiple_of(h * 512, 512)
            return mm(v_bf, B[pl.ds(at, 512), :], NT)

        def observe(st, h, c):
            for half in range(2):
                acc = None
                for s in range(4):
                    idx = jnp.broadcast_to(offS[s, pl.ds(h, 1), :], (8, 128))
                    w = wS[s, pl.ds(h, 1), :]
                    val = None
                    for q in range(4):
                        one = lanes_of(st[8 * half : 8 * half + 8, 128 * q : 128 * q + 128], idx)
                        val = one if q == 0 else jnp.where(lane_group == q, one, val)
                    acc = val * w if s == 0 else acc + val * w
                at = c * 256 + half * 128 + (h - c * PART_H)
                partial[t, pl.ds(at, 8, stride=16), :] = acc

        def rs_copy(c, d):
            peer = lax.rem(m + d, n_mode)
            return pltpu.make_async_remote_copy(
                src_ref=partial.at[t, pl.ds(c * 256 + 32 * peer, 32)],
                dst_ref=rs_in.at[t, pl.ds(c * 224 + 32 * (d - 1), 32)],
                send_sem=rs_send.at[t, c],
                recv_sem=rs_recv.at[t, c],
                device_id=(g, peer),
                device_id_type=MESH,
            )

        for c in range(PARTS):
            if t == 0:
                for i in range(LOADS // PARTS):
                    load(c * (LOADS // PARTS) + i).wait()

            def step(i, st):
                h = c * PART_H + i
                nxt = state(h + 1)
                observe(st, h, c)
                return nxt

            st = lax.fori_loop(0, PART_H - 1, step, state(c * PART_H), unroll=3)
            observe(st, c * PART_H + PART_H - 1, c)
            if t == 0 and c == 0:
                pl.semaphore_wait(barrier, n_mode + n_grid - 2)
            for d in range(1, n_mode):
                rs_copy(c, d).start()

        if t == 0:
            lax.fori_loop(0, 64, stencil_matrix, 0, unroll=2)

        hi = [hiJ[8 * i : 8 * i + 8, :] for i in range(4)]
        lo = [loJ[8 * i : 8 * i + 8, :] for i in range(4)]
        got = tuple([jnp.zeros((8, 128), F32)] * 8)
        for c in range(PARTS):
            whole = rs_in.at[t, pl.ds(c * 224, 224)]
            pltpu.make_async_copy(whole, whole, rs_recv.at[t, c]).wait()
            total = partial[t, pl.ds(pl.multiple_of(c * 256 + 32 * m, 32), 32), :]
            for d in range(n_mode - 1):
                total = total + rs_in[t, pl.ds(c * 224 + 32 * d, 32), :]
            X[pl.ds(c * 32, 32), :] = total

            def to_drifters(i, got):
                h = c * PART_H + i
                new = list(got)
                here = [hi[k] == h for k in range(4)]
                for p in range(2):
                    row = jnp.broadcast_to(X[pl.ds(c * 32 + 16 * p + i, 1), :], (8, 128))
                    for k in range(4):
                        new[4 * p + k] = jnp.where(here[k], lanes_of(row, lo[k]), got[4 * p + k])
                return tuple(new)

            got = lax.fori_loop(0, PART_H, to_drifters, got, unroll=4)
        for p in range(2):
            for k in range(4):
                val = got[4 * p + k] * gainJ[8 * k : 8 * k + 8, :]
                for q in range(4):
                    Z[t, 4 * k + q, 2 * p : 2 * p + 2, :] = val[2 * q : 2 * q + 2]

        def grid_copy(d, src, dst, send, recv):
            peer = lax.rem(g + d, n_grid)
            return pltpu.make_async_remote_copy(
                src_ref=src.at[t, peer],
                dst_ref=dst.at[t, g],
                send_sem=send.at[t],
                recv_sem=recv.at[t],
                device_id=(peer, m),
                device_id_type=MESH,
            )

        def wait_bytes(ref, sem):
            pltpu.make_async_copy(ref, ref, sem).wait()

        for d in range(1, n_grid):
            grid_copy(d, Z, R, a1_send, a1_recv).start()
        R[t, g] = Z[t, g]
        wait_bytes(R.at[t, pl.ds(0, n_grid - 1)], a1_recv.at[t])
        obs = [R[t, l] for l in range(16)]
        for k in range(16):
            acc = prec[k, 0] * obs[0]
            for l in range(1, 16):
                acc = acc + prec[k, l] * obs[l]
            C[t, k] = acc
        for d in range(1, n_grid):
            grid_copy(d, C, D, a2_send, a2_recv).start()
        D[t, g] = C[t, g]
        wait_bytes(D.at[t, pl.ds(0, n_grid - 1)], a2_recv.at[t])

        want = [jrowS[8 * i : 8 * i + 8, :] for i in range(8)]
        lane = [jlaneS[8 * i : 8 * i + 8, :] for i in range(8)]

        def to_slots(i, got):
            new = list(got)
            for r in range(2):
                jr = 2 * i + r
                here = [want[k] == jr for k in range(8)]
                gain = gainJ[pl.ds(jr, 1), :]
                for p in range(2):
                    row = D[t, i, 2 * p + r : 2 * p + r + 1, :] * gain
                    row = jnp.broadcast_to(row, (8, 128))
                    for k in range(8):
                        new[8 * p + k] = jnp.where(
                            here[k], lanes_of(row, lane[k]), new[8 * p + k]
                        )
            return tuple(new)

        got = lax.fori_loop(0, 16, to_slots, tuple([jnp.zeros((8, 128), F32)] * 16), unroll=2)
        for p in range(2):
            for k in range(8):
                S[t, pl.ds((k // 2) * 32 + 16 * p + 8 * (k % 2), 8), :] = got[8 * p + k]

        def ag_copy(c, d):
            return pltpu.make_async_remote_copy(
                src_ref=S.at[t, pl.ds(c * 32, 32)],
                dst_ref=Fw.at[t, pl.ds(c * 256 + 32 * m, 32)],
                send_sem=ag_send.at[t, c],
                recv_sem=ag_recv.at[t, c],
                device_id=(g, lax.rem(m + d, n_mode)),
                device_id_type=MESH,
            )

        for c in range(PARTS):
            for d in range(1, n_mode):
                ag_copy(c, d).start()
        for c in range(PARTS):
            own = pl.ds(pl.multiple_of(c * 256 + 32 * m, 32), 32)
            Fw[t, own, :] = S[t, pl.ds(c * 32, 32), :]

        def spread(h, c):
            lhs = []
            for half in range(2):
                at = c * 256 + half * 128 + (h - c * PART_H)
                lhs.append(Fw[t, pl.ds(at, 8, stride=16), :])
            val = jnp.concatenate(lhs, axis=0)
            v_hi = val.astype(BF16).astype(F32)
            v_lo = val - v_hi
            his = [jnp.where(group16 == q, v_hi, 0.0) for q in range(4)]
            los = [jnp.where(group16 == q, v_lo, 0.0) for q in range(4)]
            his = jnp.concatenate(his, axis=0).astype(BF16)
            los = jnp.concatenate(los, axis=0).astype(BF16)
            at = pl.multiple_of(h * 128, 128)
            mat = WT[pl.ds(at, 128), :]
            both = jnp.concatenate([his, his], axis=1)
            adj = mm(both, mat, NT) + mm(los, mat[:, :128], NT)
            adj = jnp.concatenate([adj[16 * q : 16 * q + 16] for q in range(4)], axis=1)
            return adj.astype(BF16)

        def project(adj, h):
            at = pl.multiple_of(h * 512, 512)
            return mm(adj, B[pl.ds(at, 512), :], NN)

        acc = jnp.zeros((16, 256), F32)
        for c in range(PARTS):
            wait_bytes(Fw.at[t, pl.ds(c * 256, 224)], ag_recv.at[t, c])

            def back(i, carry):
                acc, adj = carry
                h = c * PART_H + i
                nxt = spread(h + 1, c)
                return acc + project(adj, h), nxt

            acc, adj = lax.fori_loop(
                0, PART_H - 1, back, (acc, spread(c * PART_H, c)), unroll=3
            )
            acc = acc + project(adj, c * PART_H + PART_H - 1)
        acc_out[t] = acc

        for d in range(1, n_grid):
            peer = lax.rem(g + d, n_grid)
            pltpu.make_async_remote_copy(
                src_ref=acc_out.at[t],
                dst_ref=ar_in.at[t, g],
                send_sem=ar_send.at[t],
                recv_sem=ar_recv.at[t],
                device_id=(peer, m),
                device_id_type=MESH,
            ).start()
        ar_in[t, g] = acc
        wait_bytes(ar_in.at[t, pl.ds(0, n_grid - 1)], ar_recv.at[t])
        total = ar_in[t, 0]
        for l in range(1, n_grid):
            total = total + ar_in[t, l]
        total = vec[...] + total
        vec[...] = total
        out[...] = total

    hessian(0, out1)
    hessian(1, out2)

    for t in range(2):
        for c in range(PARTS):
            for sem in (rs_send, ag_send):
                piece = rs_in.at[t, pl.ds(c * 224, 224)]
                pltpu.make_async_copy(piece, piece, sem.at[t, c]).wait()
        for ref, sem in ((R, a1_send), (D, a2_send), (ar_in, ar_send)):
            piece = ref.at[t, pl.ds(0, n_grid - 1)]
            pltpu.make_async_copy(piece, piece, sem.at[t]).wait()


def local(
    pod_basis,
    probe_vectors,
    drifter_tiles,
    tile_counts,
    stencil_offsets,
    stencil_weights,
    error_scales,
    time_precision,
    *,
    n_grid,
    n_mode,
):
    vmem = pl.BlockSpec(memory_space=pltpu.VMEM)
    dma = pltpu.SemaphoreType.DMA
    table = pltpu.VMEM((64, 128), I32)
    drift_f = pltpu.VMEM((32, 128), F32)
    drift_i = pltpu.VMEM((32, 128), I32)
    return pl.pallas_call(
        functools.partial(kernel, n_grid, n_mode),
        out_shape=(jax.ShapeDtypeStruct(probe_vectors.shape, F32),) * 2,
        in_specs=[
            pl.BlockSpec(memory_space=pl.ANY),
            vmem,
            vmem,
            vmem,
            vmem,
            vmem,
            vmem,
            pl.BlockSpec(memory_space=pltpu.SMEM),
        ],
        out_specs=(vmem, vmem),
        scratch_shapes=[
            pltpu.VMEM(pod_basis.shape, BF16),
            pltpu.VMEM((64 * 128, 256), BF16),
            pltpu.VMEM((4, 64, 128), I32),
            pltpu.VMEM((4, 64, 128), F32),
            table,
            table,
            drift_i,
            drift_i,
            drift_f,
            drift_i,
            pltpu.VMEM((2, 1024, 128), F32),
            pltpu.VMEM((2, 896, 128), F32),
            pltpu.VMEM((128, 128), F32),
            pltpu.VMEM((2, 16, 4, 128), F32),
            pltpu.VMEM((2, 16, 4, 128), F32),
            pltpu.VMEM((2, 16, 4, 128), F32),
            pltpu.VMEM((2, 16, 4, 128), F32),
            pltpu.VMEM((2, 128, 128), F32),
            pltpu.VMEM((2, 1024, 128), F32),
            pltpu.VMEM((2, 16, 256), F32),
            pltpu.VMEM((2, 16, 16, 256), F32),
            pltpu.VMEM((16, 256), F32),
            dma((LOADS,)),
            dma((2, PARTS)),
            dma((2, PARTS)),
            dma((2,)),
            dma((2,)),
            dma((2,)),
            dma((2,)),
            dma((2, PARTS)),
            dma((2, PARTS)),
            dma((2,)),
            dma((2,)),
        ],
        compiler_params=pltpu.CompilerParams(
            collective_id=0, has_side_effects=True, vmem_limit_bytes=40 * 1024 * 1024
        ),
    )(
        pod_basis,
        probe_vectors,
        drifter_tiles,
        tile_counts.reshape(1, -1),
        stencil_offsets,
        stencil_weights,
        error_scales,
        time_precision,
    )


def solution(mesh):
    return jax.shard_map(
        functools.partial(local, n_grid=mesh.shape["grid"], n_mode=mesh.shape["mode"]),
        mesh=mesh,
        in_specs=(
            P("grid", "mode"),
            P(None, "mode"),
            P("grid", None),
            P("grid"),
            P(None, "grid", None),
            P(None, "grid", None),
            P("grid", None),
            P(),
        ),
        out_specs=(P(None, "mode"), P(None, "mode")),
        check_vma=False,
    )
```

time: 792 us -> 110 us (0.14); the launches traced: 783 us -> 110 us
  waiting for transfers between devices: 263 us -> 0 us
  other arithmetic: 203 us -> 0 us
  local copies, waits for them, and re-layouts: 128 us -> 6.41 us
  Pallas kernels: 0 us -> 103 us
  blocking collectives: 101 us -> 0 us
  matrix products: 72.6 us -> 0 us
  between operations: 14.2 us -> 0.66 us
    psum x2 -> x0, waiting for transfers between devices: 182 us -> none  [hessian(): scaled = lax.psum(scaled, 'mode')]
    scatter-add x2 -> x0, other arithmetic: 173 us -> none  [hessian(): jnp.zeros((probe_count, row_span), jnp.float32).at[:, safe_rows.reshape(-1)]]
    gather x2 -> x0, local copies, waits for them, and re-layouts: 120 us -> none  [hessian(): state_rows[:, safe_rows]]
    pallas_call x0 -> x1, Pallas kernels: none -> 103 us  [local(): pl.pallas_call(functools.partial(kernel, n_grid, n_mode), out_shape=(jax....]
    psum x2 -> x0, blocking collectives: 101 us -> none  [hessian(): increment = lax.psum(partial_back, 'grid')]
    all_gather x2 -> x0, waiting for transfers between devices: 81.7 us -> none  [hessian(): lax.all_gather(scaled[None], 'grid', axis=0, tiled=True)]
    dot_general x7 -> x0, matrix products: 72.6 us -> none  [the longest x2 32 us: hessian(): lax.dot_general(probe_bf, pod_basis, (((1,), (1,)), ((), ())), preferred_...]
    mul x5 -> x0, other arithmetic: 10.7 us -> none  [the longest x2 8.77 us: hessian(): spread = (live_weight[None] * weighted[:, None, :]).reshape(probe_count, -1)]
  transfers between devices with their start and end apart: 4 -> 0, of which waited for: 4 -> 0; matrix products, arithmetic and copies ran while one was open for 0% -> 0% of each run, Pallas kernels for 0% -> 0%
where the time goes in v1:
time: 110 us
  Pallas kernels  103 us (94%)
  local copies, waits for them, and re-layouts  6.41 us (6%)
    pallas_call x1, Pallas kernels, local(): pl.pallas_call(functools.partial(kernel, n_grid, n_mode), out_shape=(jax....  103 us
    unnamed x16, local copies, waits for them, and re-layouts  6.41 us

profile of v1, /device:TPU:1, one launch (start us, length us, event | category | flops | bytes accessed | tf_op | source)
XLA Modules:
  0.0 110.0 jit_solution(11011847431659065910)
XLA Ops:
  0.6 0.0 copy-start
  0.6 0.8 copy-done
  1.5 0.0 copy-start.1
  1.5 0.8 copy-done.1
  2.3 0.0 copy-start.2
  2.3 0.7 copy-done.2
  3.0 0.0 copy-start.3
  3.0 0.7 copy-done.3
  3.7 0.0 copy-start.4
  3.8 0.7 copy-done.4
  4.5 0.0 copy-start.5
  4.5 0.7 copy-done.5
  5.2 0.0 copy-start.6
  5.2 0.7 copy-done.6
  5.8 103.0 %shard_map.95 = (f32[16,256]{1,0:T(8,128)S(1)}, f32[16,256]{1,0:T(8,128)S(1)}) custom-call(bf16[32768,256]{1,0:T(8,128)(2,1)} %basis.1, f32[16,256]{1,0:T(8,128)S(1)} %copy-done.2, s32[1,4096]{1,0:T(1,128)S(1)} %copy-done.3, s32[1,256]{1,0:T(1,128)S(1)} %bitcast.1, s32[4,1,4096]{2,1,0:T(1,128)S(1)} %copy-done, f32[4,1,4096]{2,1,0:T(1,128)S(1)} %copy-done.1, ...), custom_call_target="tpu_custom_call" | custom-call | tf_op jit(solution)/shard_map/pallas_call | solution.py:419
  108.8 0.6 copy.12
  109.4 0.6 copy.13
Async XLA Ops:
  0.6 0.8 copy-start
  1.5 0.8 copy-start.1
  2.3 0.7 copy-start.2
  3.0 0.7 copy-start.3
  3.7 0.7 copy-start.4
  4.5 0.7 copy-start.5
  5.2 0.7 copy-start.6

commit v2 on v1

v2 whole, which is shorter than its diff:
```python
import functools

import jax
import jax.numpy as jnp
from jax import lax
from jax.experimental import pallas as pl
from jax.experimental.pallas import tpu as pltpu
from jax.sharding import PartitionSpec as P

F32 = jnp.float32
BF16 = jnp.bfloat16
I32 = jnp.int32
MESH = pl.DeviceIdType.MESH

LOADS = 16
GROUP = 4

NN = (((1,), (0,)), ((), ()))
NT = (((1,), (1,)), ((), ()))


def mm(a, b, dims):
    return lax.dot_general(a, b, dims, preferred_element_type=F32)


def lanes_of(x, idx):
    return jnp.take_along_axis(x, idx, axis=1, mode="promise_in_bounds")


def split(x):
    hi = x.astype(BF16)
    return hi, (x - hi.astype(F32)).astype(BF16)


def kernel(
    n_grid,
    n_mode,
    basis,
    probe_hbm,
    tiles_hbm,
    counts_hbm,
    offs_hbm,
    wts_hbm,
    scales_hbm,
    prec_hbm,
    out1,
    out2,
    B,
    WT,
    tiles,
    counts,
    offs,
    wts,
    scales,
    prec,
    offS,
    wS,
    jrowS,
    jlaneS,
    hiJ,
    gainJ,
    packJ,
    lowJ,
    partial,
    parts,
    Z,
    R,
    C,
    D,
    Y,
    acc_out,
    ar_in,
    vec,
    load_sem,
    small_sem,
    e1_send,
    e1_recv,
    e2_send,
    e2_recv,
    ar_send,
    ar_recv,
):
    g = lax.axis_index("grid")
    m = lax.axis_index("mode")
    n_all = n_grid * n_mode
    me = g * n_mode + m
    rows = basis.shape[0] // LOADS

    small = [
        pltpu.make_async_copy(src, dst, small_sem.at[i])
        for i, (src, dst) in enumerate(
            (
                (tiles_hbm, tiles),
                (counts_hbm, counts),
                (offs_hbm, offs),
                (scales_hbm, scales),
                (wts_hbm, wts),
                (probe_hbm, vec),
                (prec_hbm, prec),
            )
        )
    ]
    for copy in small:
        copy.start()

    def load(i):
        return pltpu.make_async_copy(
            basis.at[pl.ds(i * rows, rows)], B.at[pl.ds(i * rows, rows)], load_sem.at[i]
        )

    for i in range(LOADS):
        load(i).start()

    def window_at(i):
        far = i // 4
        dy = jnp.where(far == 0, 2, jnp.where(far == 1, 1, jnp.where(far == 2, 3, 0)))
        dz = 1 - (i // 2) % 2
        dc = 1 - i % 2
        z = (g // 8 + dz) % 2
        y = ((g // 2) % 4 + dy) % 4
        return z * 8 + y * 2 + (g + dc) % 2

    def mode_at(dx, dz):
        return ((m // 4 + dz) % 2) * 4 + (m % 4 + dx) % 4

    modes = [mode_at(dx, dz) for dx, dz in ((2, 1), (1, 1), (3, 1), (0, 1), (2, 0), (1, 0), (3, 0))]

    barrier = pltpu.get_barrier_semaphore()

    def greet(i):
        there = window_at(i)
        for peer in modes + ([m] if i < n_grid - 1 else []):
            pl.semaphore_signal(barrier, inc=1, device_id=(there, peer), device_id_type=MESH)

    for copy in small:
        copy.wait()
    sub = lax.broadcasted_iota(I32, (256, 256), 0)
    lan = lax.broadcasted_iota(I32, (256, 256), 1)
    upto = (sub <= lan).astype(BF16)
    ones = jnp.ones((16, 256), BF16)
    base = jnp.zeros((16, 256), F32)
    first = lax.broadcasted_iota(I32, (16, 256), 0) == 0
    count_row = jnp.broadcast_to(counts[...].astype(F32), (16, 256))
    inverse = jnp.zeros((64, 256), F32)
    hsub = lax.broadcasted_iota(I32, (64, 256), 0)
    lsub = lax.broadcasted_iota(I32, (128, 256), 0)
    jlan = lax.broadcasted_iota(I32, (1, 256), 1)
    for b in range(16):
        greet(b)
        cols = pl.ds(b * 256, 256)
        lt = tiles[0:1, cols] - g * 256
        onehot = (sub == lt).astype(F32)
        onehot_bf = onehot.astype(BF16)
        within = mm(onehot_bf, upto, NN)
        looked = mm(jnp.where(first, base, count_row).astype(BF16), onehot_bf, NN)
        rank = jnp.sum(onehot * within, axis=0, keepdims=True) + looked[0:1] - 1.0
        base = base + mm(ones, onehot_bf, NT)
        hi = lt >> 2
        lo = (lt & 3) * 32 + rank.astype(I32)
        hiJ[0:1, cols] = hi
        gainJ[0:1, cols] = scales[0:1, cols] / jnp.sqrt(looked[1:2])
        packed = offs[0, 0:1, cols]
        for s in range(1, 4):
            packed = packed | (offs[s, 0:1, cols] << (7 * s))
        packJ[0:1, cols] = packed
        j = jlan + b * 256
        low = lsub == lo
        lowJ[:, cols] = low.astype(F32).astype(BF16)
        jrow1 = jnp.where(low, ((j >> 7) + 1).astype(F32), 0.0).astype(BF16)
        jlane = jnp.where(low, (j & 127).astype(F32), 0.0).astype(BF16)
        high = (hsub == hi).astype(F32).astype(BF16)
        inverse = inverse + mm(high, jnp.concatenate([jrow1, jlane], axis=0), NT)
    jrowS[...] = inverse[:, :128].astype(I32) - 1
    jlaneS[...] = inverse[:, 128:].astype(I32)

    for half in range(2):
        at = [32 * half + 8 * i for i in range(4)]
        want = [jrowS[a : a + 8, :] for a in at]
        lane = [jlaneS[a : a + 8, :] for a in at]

        def place(r, got):
            cols = pl.ds(pl.multiple_of(r * 128, 128), 128)
            src = [packJ[0:1, cols]] + [wts[s, 0:1, cols] for s in range(4)]
            src = [jnp.broadcast_to(x, (8, 128)) for x in src]
            new = []
            for i in range(4):
                here = want[i] == r
                for k in range(5):
                    new.append(jnp.where(here, lanes_of(src[k], lane[i]), got[5 * i + k]))
            return tuple(new)

        zero = [jnp.zeros((8, 128), I32)] + [jnp.zeros((8, 128), F32)] * 4
        got = lax.fori_loop(0, 32, place, tuple(zero * 4), unroll=2)
        for i in range(4):
            for s in range(4):
                offS[s, pl.ds(at[i], 8), :] = (got[5 * i] >> (7 * s)) & 127
                wS[s, pl.ds(at[i], 8), :] = got[5 * i + 1 + s]

    def stencil_matrix(h, carry):
        point = lax.broadcasted_iota(I32, (128, 128), 0)
        w = jnp.zeros((128, 128), F32)
        for s in range(4):
            w = w + jnp.where(point == offS[s, pl.ds(h, 1), :], wS[s, pl.ds(h, 1), :], 0.0)
        w_hi, w_lo = split(w)
        at = pl.multiple_of(h * 128, 128)
        WT[pl.ds(at, 128), 0:128] = w_hi
        WT[pl.ds(at, 128), 128:256] = w_lo
        return carry

    lane_group = lax.broadcasted_iota(I32, (8, 128), 1) >> 5
    group16 = lax.broadcasted_iota(I32, (16, 128), 1) >> 5

    def wait_bytes(ref, sem):
        pltpu.make_async_copy(ref, ref, sem).wait()

    def hessian(t, out):
        v_bf = vec[...].astype(BF16)

        def state(n):
            at = pl.multiple_of(n * GROUP * 512, GROUP * 512)
            return mm(v_bf, B[pl.ds(at, GROUP * 512), :], NT)

        def observe(st, n):
            for k in range(GROUP):
                h = n * GROUP + k
                for half in range(2):
                    acc = None
                    for s in range(4):
                        idx = jnp.broadcast_to(offS[s, pl.ds(h, 1), :], (8, 128))
                        w = wS[s, pl.ds(h, 1), :]
                        val = None
                        for q in range(4):
                            at = 512 * k + 128 * q
                            one = lanes_of(st[8 * half : 8 * half + 8, at : at + 128], idx)
                            val = one if q == 0 else jnp.where(lane_group == q, one, val)
                        acc = val * w if s == 0 else acc + val * w
                    at = (h // 16) * 256 + half * 128 + h % 16
                    partial[pl.ds(at, 8, stride=16), :] = acc

        def step(n, st):
            if t == 0:
                load(n + 1).wait()
            nxt = state(n + 1)
            observe(st, n)
            return nxt

        if t == 0:
            load(0).wait()
        st = lax.fori_loop(0, LOADS - 1, step, state(0))
        observe(st, LOADS - 1)

        p_hi, p_lo = split(partial[...])
        parts[:, 0:128] = p_hi
        parts[:, 128:256] = p_lo
        if t == 0:
            pl.semaphore_wait(barrier, n_all - 1)

        def send_piece(there, peer):
            at = there * n_mode + peer
            pltpu.make_async_remote_copy(
                src_ref=Z.at[t, at],
                dst_ref=R.at[t, me],
                send_sem=e1_send.at[t],
                recv_sem=e1_recv.at[t],
                device_id=(there, peer),
                device_id_type=MESH,
            ).start()

        def to_drifters(i, carry):
            there = window_at(i)
            cols = pl.ds(pl.multiple_of(there * 256, 256), 256)
            low = lowJ[:, cols]
            picked = mm(parts[...], jnp.concatenate([low, low], axis=0), NN)
            mask = (lax.broadcasted_iota(I32, (64, 256), 0) == hiJ[0:1, cols]).astype(F32)
            picked = picked.reshape(4, 16, 16, 256) * mask.reshape(4, 1, 16, 256)
            val = jnp.sum(jnp.sum(picked, axis=0), axis=1)
            val = val * gainJ[0:1, cols]
            for k in range(n_mode):
                for r in range(2):
                    Z[t, there * n_mode + k, 2 * r : 2 * r + 2, :] = val[
                        2 * k : 2 * k + 2, 128 * r : 128 * r + 128
                    ]
            for peer in modes:
                send_piece(there, peer)

            @pl.when(i < n_grid - 1)
            def _():
                send_piece(there, m)

            return carry

        lax.fori_loop(0, n_grid, to_drifters, 0)
        R[t, me] = Z[t, me]

        if t == 0:
            lax.fori_loop(0, 64, stencil_matrix, 0, unroll=2)

        wait_bytes(R.at[t, pl.ds(0, n_all - 1)], e1_recv.at[t])
        obs = []
        for l in range(16):
            total = R[t, l * n_mode]
            for k in range(1, n_mode):
                total = total + R[t, l * n_mode + k]
            obs.append(total)

        def couple(i, carry):
            there = window_at(i)
            terms = [prec[there, l] * obs[l] for l in range(16)]
            while len(terms) > 1:
                terms = [a + b for a, b in zip(terms[::2], terms[1::2])]
            C[t, there] = terms[0]

            def send_back(peer):
                pltpu.make_async_remote_copy(
                    src_ref=C.at[t, there],
                    dst_ref=D.at[t, me],
                    send_sem=e2_send.at[t],
                    recv_sem=e2_recv.at[t],
                    device_id=(there, peer),
                    device_id_type=MESH,
                ).start()

            for peer in modes:
                send_back(peer)

            @pl.when(i < n_grid - 1)
            def _():
                send_back(m)

            return carry

        lax.fori_loop(0, n_grid, couple, 0)
        D[t, me] = C[t, g]
        wait_bytes(D.at[t, pl.ds(0, n_all - 1)], e2_recv.at[t])

        def gather_rows(i, carry):
            for r in range(2):
                cols = pl.ds(pl.multiple_of((2 * i + r) * 128, 128), 128)
                gain = gainJ[0:1, cols]
                for k in range(n_mode):
                    val = D[t, i * n_mode + k, 2 * r : 2 * r + 2, :]
                    Y[pl.ds(i * 32 + 16 * r + 2 * k, 2), :] = val * gain
            return carry

        lax.fori_loop(0, n_grid, gather_rows, 0, unroll=2)

        def slots(h):
            row = jnp.broadcast_to(jrowS[pl.ds(h, 1), :], (8, 128))
            idx = jnp.broadcast_to(jlaneS[pl.ds(h, 1), :], (8, 128))
            got = [jnp.zeros((8, 128), F32)] * 2
            for jr in range(32):
                here = row == jr
                for half in range(2):
                    src = Y[16 * jr + 8 * half : 16 * jr + 8 * half + 8, :]
                    got[half] = jnp.where(here, lanes_of(src, idx), got[half])
            return jnp.concatenate(got, axis=0)

        def spread(val, h):
            v_hi = val.astype(BF16).astype(F32)
            v_lo = val - v_hi
            his = [jnp.where(group16 == q, v_hi, 0.0) for q in range(4)]
            los = [jnp.where(group16 == q, v_lo, 0.0) for q in range(4)]
            his = jnp.concatenate(his, axis=0).astype(BF16)
            los = jnp.concatenate(los, axis=0).astype(BF16)
            at = pl.multiple_of(h * 128, 128)
            mat = WT[pl.ds(at, 128), :]
            both = jnp.concatenate([his, his], axis=1)
            los = jnp.concatenate([los, jnp.zeros_like(los)], axis=1)
            adj = mm(jnp.concatenate([both, los], axis=0), mat, NT)
            adj = adj[:64] + adj[64:]
            adj = jnp.concatenate([adj[16 * q : 16 * q + 16] for q in range(4)], axis=1)
            return adj.astype(BF16)

        def project(adj, n):
            at = pl.multiple_of(n * GROUP * 512, GROUP * 512)
            return mm(adj, B[pl.ds(at, GROUP * 512), :], NN)

        def spreads(vals, n):
            return jnp.concatenate(
                [spread(vals[k], n * GROUP + k) for k in range(GROUP)], axis=1
            )

        def slot_rows(n):
            return tuple(slots(n * GROUP + k) for k in range(GROUP))

        last = 64 // GROUP - 1

        def back(n, carry):
            acc, adj, vals = carry
            acc = acc + project(adj, n)
            nxt = spreads(vals, n + 1)
            return acc, nxt, slot_rows(jnp.minimum(n + 2, last))

        start = (jnp.zeros((16, 256), F32), spreads(slot_rows(0), 0), slot_rows(1))
        acc, adj, _ = lax.fori_loop(0, last, back, start)
        acc = acc + project(adj, last)
        acc_out[t] = acc

        def send_sum(i, carry):
            pltpu.make_async_remote_copy(
                src_ref=acc_out.at[t],
                dst_ref=ar_in.at[t, g],
                send_sem=ar_send.at[t],
                recv_sem=ar_recv.at[t],
                device_id=(window_at(i), m),
                device_id_type=MESH,
            ).start()
            return carry

        lax.fori_loop(0, n_grid - 1, send_sum, 0)
        ar_in[t, g] = acc
        wait_bytes(ar_in.at[t, pl.ds(0, n_grid - 1)], ar_recv.at[t])
        total = ar_in[t, 0]
        for l in range(1, n_grid):
            total = total + ar_in[t, l]
        total = vec[...] + total
        vec[...] = total
        out[...] = total

    hessian(0, out1)
    hessian(1, out2)

    for t in range(2):
        wait_bytes(R.at[t, pl.ds(0, n_all - 1)], e1_send.at[t])
        wait_bytes(D.at[t, pl.ds(0, n_all - 1)], e2_send.at[t])
        wait_bytes(ar_in.at[t, pl.ds(0, n_grid - 1)], ar_send.at[t])


def local(
    pod_basis,
    probe_vectors,
    drifter_tiles,
    tile_counts,
    stencil_offsets,
    stencil_weights,
    error_scales,
    time_precision,
    *,
    n_grid,
    n_mode,
):
    vmem = pl.BlockSpec(memory_space=pltpu.VMEM)
    hbm = pl.BlockSpec(memory_space=pltpu.HBM)
    dma = pltpu.SemaphoreType.DMA
    table = pltpu.VMEM((64, 128), I32)
    n_all = n_grid * n_mode
    return pl.pallas_call(
        functools.partial(kernel, n_grid, n_mode),
        out_shape=(jax.ShapeDtypeStruct(probe_vectors.shape, F32),) * 2,
        in_specs=[hbm] * 8,
        out_specs=(vmem, vmem),
        scratch_shapes=[
            pltpu.VMEM(pod_basis.shape, BF16),
            pltpu.VMEM((64 * 128, 256), BF16),
            pltpu.VMEM((1, 4096), I32),
            pltpu.VMEM((1, 256), I32),
            pltpu.VMEM((4, 1, 4096), I32),
            pltpu.VMEM((4, 1, 4096), F32),
            pltpu.VMEM((1, 4096), F32),
            pltpu.SMEM((16, 16), F32),
            pltpu.VMEM((4, 64, 128), I32),
            pltpu.VMEM((4, 64, 128), F32),
            table,
            table,
            pltpu.VMEM((1, 4096), I32),
            pltpu.VMEM((1, 4096), F32),
            pltpu.VMEM((1, 4096), I32),
            pltpu.VMEM((128, 4096), BF16),
            pltpu.VMEM((1024, 128), F32),
            pltpu.VMEM((1024, 256), BF16),
            pltpu.VMEM((2, n_all, 4, 128), F32),
            pltpu.VMEM((2, n_all, 4, 128), F32),
            pltpu.VMEM((2, n_grid, 4, 128), F32),
            pltpu.VMEM((2, n_all, 4, 128), F32),
            pltpu.VMEM((512, 128), F32),
            pltpu.VMEM((2, 16, 256), F32),
            pltpu.VMEM((2, n_grid, 16, 256), F32),
            pltpu.VMEM((16, 256), F32),
            dma((LOADS,)),
            dma((7,)),
            dma((2,)),
            dma((2,)),
            dma((2,)),
            dma((2,)),
            dma((2,)),
            dma((2,)),
        ],
        compiler_params=pltpu.CompilerParams(
            collective_id=0, has_side_effects=True, vmem_limit_bytes=64 * 1024 * 1024
        ),
    )(
        pod_basis,
        probe_vectors,
        drifter_tiles,
        tile_counts.reshape(1, -1),
        stencil_offsets,
        stencil_weights,
        error_scales,
        time_precision,
    )


def solution(mesh):
    return jax.shard_map(
        functools.partial(local, n_grid=mesh.shape["grid"], n_mode=mesh.shape["mode"]),
        mesh=mesh,
        in_specs=(
            P("grid", "mode"),
            P(None, "mode"),
            P("grid", None),
            P("grid"),
            P(None, "grid", None),
            P(None, "grid", None),
            P("grid", None),
            P(),
        ),
        out_specs=(P(None, "mode"), P(None, "mode")),
        check_vma=False,
    )
```

time: 110 us -> 96.5 us (0.88)
  Pallas kernels: 103 us -> 92.9 us
  local copies, waits for them, and re-layouts: 6.41 us -> 2.65 us
    pallas_call x1, Pallas kernels: 103 us -> 92.9 us  [local(): pl.pallas_call(functools.partial(kernel, n_grid, n_mode), out_shape=(jax....]
    unnamed x16 -> x2, local copies, waits for them, and re-layouts: 6.41 us -> 2.65 us
where the time goes in v2:
time: 96.5 us; the launch traced here: 96.2 us
  Pallas kernels  92.9 us (96%)
  local copies, waits for them, and re-layouts  2.65 us (3%)
    pallas_call x1, Pallas kernels, local(): pl.pallas_call(functools.partial(kernel, n_grid, n_mode), out_shape=(jax....  92.9 us
    unnamed x2, local copies, waits for them, and re-layouts  2.65 us

profile of v2, /device:TPU:1, one launch (start us, length us, event | category | flops | bytes accessed | tf_op | source)
XLA Modules:
  0.0 96.2 jit_solution(17230130855136722644)
XLA Ops:
  0.6 92.9 %shard_map.95 = (f32[16,256]{1,0:T(8,128)}, f32[16,256]{1,0:T(8,128)}) custom-call(bf16[32768,256]{1,0:T(8,128)(2,1)} %basis.1, f32[16,256]{1,0:T(8,128)} %probe_hbm.1, s32[1,4096]{1,0:T(1,128)} %tiles_hbm.1, s32[1,256]{1,0:T(1,128)} %bitcast.1, s32[4,1,4096]{2,1,0:T(1,128)} %offs_hbm.1, f32[4,1,4096]{2,1,0:T(1,128)} %wts_hbm.1, f32[1,4096]{1,0:T(1,128)} %scales_hbm.1, ...), custom_call_target="tpu_custom_call" | custom-call | tf_op jit(solution)/shard_map/pallas_call | solution.py:447
  93.5 1.3 %copy.12 = f32[16,256]{1,0:T(8,128)} copy(f32[16,256]{1,0:T(8,128)} %get-tuple-element.4) | data formatting | bytes 32768
  94.9 1.3 %copy.13 = f32[16,256]{1,0:T(8,128)} copy(f32[16,256]{1,0:T(8,128)} %get-tuple-element.5) | data formatting | bytes 32768
